TPU v7x, 128 devices: a whole 4x4x4 slice. The times are simulated.
128 devices in a mesh: grp: 16 (over z, y_lo, core), tp: 8 (over x, y_hi).
Axes of the slice: x: 4, y: 4 (y_hi: 2, y_lo: 2; y = y_hi * 2 + y_lo), z: 4, core: 2. Of those that a mesh axis runs over, the one named last changes fastest.
Arguments:
- hidden: bfloat16 [512, 16384], P(('grp', 'tp')), may hold values from -130 to 130
- gain: float32 [16384], replicated, may hold values from 0.5 to 1.5
- head: bfloat16 [16384, 65536], P(None, ('grp', 'tp')), may hold values from -3 to 3
Outputs:
- log_probs: float32 [512, 65536], P(('grp', 'tp'))
All inputs are finite; a program needn't handle non-finite values.
Results may differ from a plain program's by a relative error of at most 0.00055.
Values may be sent and summed in bfloat16 or wider, within the bound.
A program may use at most 128 MiB of HBM per device.

v0:
```python
import jax
import jax.numpy as jnp
from jax import lax
from jax.sharding import PartitionSpec as P


def in_order(pieces, dim):
    pieces = jnp.moveaxis(pieces, 0, dim)
    dims = pieces.shape
    return pieces.reshape(*dims[:dim], dims[dim] * dims[dim + 1], *dims[dim + 2 :])


def sent_to_all(array, axis):
    count = lax.axis_size(axis)
    return lax.all_to_all(
        jnp.broadcast_to(array[None], (count, *array.shape)), axis, 0, 0, tiled=True
    )


def collect(array, axis, dim):
    return in_order(sent_to_all(array, axis), dim)


def on_device(hidden, gain, head):
    values = hidden.astype(jnp.float32)
    mean_square = jnp.mean(values * values, axis=-1, keepdims=True)
    normed = (values * lax.rsqrt(mean_square + 1e-05) * gain).astype(jnp.bfloat16)
    group_block = collect(normed, "tp", 0)
    logits = jnp.dot(
        lax.all_gather(group_block, "grp", axis=0, tiled=True),
        head,
        preferred_element_type=jnp.float32,
    )
    owned = lax.all_to_all(logits, ("grp", "tp"), split_axis=0, concat_axis=1, tiled=True)
    top = jnp.max(owned, axis=-1, keepdims=True)
    total = jnp.sum(jnp.exp(owned - top), axis=-1, keepdims=True)
    return owned - top - jnp.log(total)


def solution(mesh):
    return jax.shard_map(
        on_device,
        mesh=mesh,
        in_specs=(P(("grp", "tp"), None), P(), P(None, ("grp", "tp"))),
        out_specs=P(("grp", "tp"), None),
        check_vma=False,
    )
```

profile of v0, /device:TPU:1, one launch (start us, length us, event | category | flops | bytes accessed | tf_op | source)
XLA Modules:
  0.0 179.9 jit_solution(17725672794546746063)
XLA Ops:
  6.5 0.0 all-gather.2.cloned.1.call-start
  6.5 1.2 fusion.2
  7.7 1.0 fusion.4
  8.7 0.3 broadcast_in_dim.2
  9.0 22.5 %all_to_all.24 = bf16[8,4,16384]{2,1,0:T(4,128)(2,1)S(1)} all-to-all(bf16[8,4,16384]{2,1,0:T(4,128)(2,1)S(1)} %broadcast_in_dim.2), channel_id=1, replica_groups=mesh['grp'=16,'tp'=8] {'tp'}, dimensions={0} | all-to-all | bytes 2097152 | tf_op jit(solution)/shard_map/all_to_all | solution.py:15
  31.6 1.1 reshape.25
  32.6 0.0 all-gather.2.cloned.1.call-update
  32.7 92.8 %all-gather.2.cloned.1.call-done = bf16[512,16384]{1,0:T(8,128)(2,1)} async-done(((bf16[32,16384]{1,0:T(8,128)(2,1)}), bf16[512,16384]{1,0:T(8,128)(2,1)}) %all-gather.2.cloned.1.call-update) | async-done | bytes 16777232 | tf_op jit(solution)/shard_map/all_gather | solution.py:30
  125.4 16.4 %fusion.5 = f32[512,512]{1,0:T(8,128)S(1)} fusion(bf16[512,16384]{1,0:T(8,128)(2,1)} %all-gather.2.cloned.1.call-done, bf16[16384,512]{1,0:T(8,128)(2,1)} %param.5), kind=kOutput, calls=%fused_computation.10 | convolution fusion | flops 8589934592 | bytes 34603008 | tf_op jit(solution)/shard_map/dot_general | solution.py:29
  141.9 0.3 all_to_all.18
  142.2 28.3 %all_to_all.25 = f32[128,4,512]{2,1,0:T(4,128)S(1)} all-to-all(f32[128,4,512]{2,1,0:T(4,128)S(1)} %all_to_all.18), channel_id=1, replica_groups=mesh['grp'=16,'tp'=8] {'grp','tp'}, dimensions={0} | all-to-all | bytes 2097152 | tf_op jit(solution)/shard_map/all_to_all | solution.py:34
  170.4 0.7 reduce_max.9
  171.1 0.7 fusion.1
  171.8 1.2 subtract_subtract_fusion
  (2 shorter events, 0.0 us)
Async XLA Ops:
  6.5 118.9 %all-gather.2.cloned.1.call-start = ((), (), s32[]{:S(2)}) async-start(), calls=%async_computation.2 | async-start | bytes 17825792 | tf_op jit(solution)/shard_map/all_gather | solution.py:30
Sparse Core Ops, SparseCore 0:
  32.8 92.5 all-gather.1
where the time goes:
time: 180 us
  waiting for transfers between devices  92.8 us (52%)
  blocking collectives  50.8 us (28%)
  matrix products  16.4 us (9%)
  between operations  13.4 us (7%)
  other arithmetic  4.83 us (3%)
    all_gather x1, waiting for transfers between devices, on_device(): lax.all_gather(group_block, 'grp', axis=0, tiled=True)  92.8 us
    all_to_all x1, blocking collectives, on_device(): lax.all_to_all(logits, ('grp', 'tp'), split_axis=0, concat_axis=1, tiled=...  28.3 us
    all_to_all x1, blocking collectives, sent_to_all(): lax.all_to_all(jnp.broadcast_to(array[None], (count, *array.shape)), axis...  22.5 us
    dot_general x1, matrix products, on_device(): jnp.dot(lax.all_gather(group_block, 'grp', axis=0, tiled=True), head, pre...  16.4 us
  transfers between devices with their start and end apart: 1, of which 1 were waited for; matrix products, arithmetic and copies ran while one was open for 0% of the time, Pallas kernels for 0%

commit v1 on v0

--- a/solution.py
+++ b/solution.py
@@ -27,7 +27,9 @@
     normed = (values * lax.rsqrt(mean_square + 1e-05) * gain).astype(jnp.bfloat16)
     group_block = collect(normed, "tp", 0)
     logits = jnp.dot(
-        lax.all_gather(group_block, "grp", axis=0, tiled=True),
+        jnp.concatenate(
+            lax.all_to_all(jnp.stack(lax.axis_size("grp") * [group_block], 0), "grp", 0, 0), 0
+        ),
         head,
         preferred_element_type=jnp.float32,
     )

time: 180 us -> 300 us (1.67)
  blocking collectives: 50.8 us -> 239 us
  waiting for transfers between devices: 92.8 us -> 0 us
  local copies, waits for them, and re-layouts: 1.68 us -> 27.8 us
  between operations: 13.4 us -> 0.05 us
  matrix products: 16.4 us -> 27.4 us
    all_to_all x0 -> x1, blocking collectives: none -> 192 us  [on_device(): lax.all_to_all(jnp.stack(lax.axis_size('grp') * [group_block], 0), 'grp',...]
    all_gather x1 -> x0, waiting for transfers between devices: 92.8 us -> none  [on_device(): lax.all_gather(group_block, 'grp', axis=0, tiled=True)]
    dot_general x0 -> x2, local copies, waits for them, and re-layouts: none -> 25.5 us  [on_device(): jnp.dot(jnp.concatenate(lax.all_to_all(jnp.stack(lax.axis_size('grp') * [...]
    dot_general x1, matrix products: 16.4 us -> 27.4 us  [on_device(): jnp.dot(jnp.concatenate(lax.all_to_all(jnp.stack(lax.axis_size('grp') * [...]
    all_to_all x1, blocking collectives: 28.3 us -> 24.7 us  [on_device(): lax.all_to_all(logits, ('grp', 'tp'), split_axis=0, concat_axis=1, tiled=...]
  transfers between devices with their start and end apart: 1 -> 0, of which waited for: 1 -> 0; matrix products, arithmetic and copies ran while one was open for 0% -> 0% of each run, Pallas kernels for 0% -> 0%
where the time goes in v1:
time: 300 us; the launch traced here: 299 us
  blocking collectives  239 us (80%)
  local copies, waits for them, and re-layouts  27.8 us (9%)
  matrix products  27.4 us (9%)
  other arithmetic  4.83 us (2%)
    all_to_all x1, blocking collectives, on_device(): lax.all_to_all(jnp.stack(lax.axis_size('grp') * [group_block], 0), 'grp',...  192 us
    dot_general x1, matrix products, on_device(): jnp.dot(jnp.concatenate(lax.all_to_all(jnp.stack(lax.axis_size('grp') * [...  27.4 us
    dot_general x2, local copies, waits for them, and re-layouts, on_device(): jnp.dot(jnp.concatenate(lax.all_to_all(jnp.stack(lax.axis_size('grp') * [...  25.5 us
    all_to_all x1, blocking collectives, on_device(): lax.all_to_all(logits, ('grp', 'tp'), split_axis=0, concat_axis=1, tiled=...  24.7 us
    all_to_all x1, blocking collectives, sent_to_all(): lax.all_to_all(jnp.broadcast_to(array[None], (count, *array.shape)), axis...  22.5 us

profile of v1, /device:TPU:1, one launch (start us, length us, event | category | flops | bytes accessed | tf_op | source)
XLA Modules:
  0.0 299.1 jit_solution(6077821142668294026)
XLA Ops:
  0.0 1.2 fusion.5
  1.2 1.0 fusion.7
  2.2 0.3 broadcast_in_dim.2
  2.5 22.5 %all_to_all.26 = bf16[8,4,16384]{2,1,0:T(4,128)(2,1)S(1)} all-to-all(bf16[8,4,16384]{2,1,0:T(4,128)(2,1)S(1)} %broadcast_in_dim.2), channel_id=1, replica_groups=mesh['grp'=16,'tp'=8] {'tp'}, dimensions={0} | all-to-all | bytes 2097152 | tf_op jit(solution)/shard_map/all_to_all | solution.py:15
  25.0 0.3 stack_reshape.2
  25.3 1.7 stack.3
  27.0 191.8 %all_to_all.27 = bf16[16,32,16384]{2,1,0:T(8,128)(2,1)} all-to-all(bf16[16,32,16384]{2,1,0:T(8,128)(2,1)S(1)} %stack.3), channel_id=1, replica_groups=mesh['grp'=16,'tp'=8] {'grp'}, dimensions={0} | all-to-all | bytes 33554432 | tf_op jit(solution)/shard_map/all_to_all | solution.py:31
  218.9 24.8 %dot_general.5 = bf16[128,4,16384]{2,1,0:T(4,128)(2,1)} reshape(bf16[16,32,16384]{2,1,0:T(8,128)(2,1)} %all_to_all.27) | data formatting | bytes 33554432 | tf_op jit(solution)/shard_map/dot_general | solution.py:29
  243.7 27.4 %fusion = f32[128,4,512]{2,0,1:T(8,128)S(1)} fusion(bf16[16384,512]{1,0:T(8,128)(2,1)} %param.5, bf16[128,4,16384]{2,1,0:T(4,128)(2,1)} %dot_general.5), kind=kOutput, calls=%fused_computation | convolution fusion | flops 8589934592 | bytes 34603008 | tf_op jit(solution)/shard_map/dot_general | solution.py:29
  271.1 0.7 copy.6
  271.8 24.7 %all_to_all.28 = f32[128,4,512]{2,1,0:T(4,128)S(1)} all-to-all(f32[128,4,512]{2,1,0:T(4,128)S(1)} %copy.6), channel_id=1, replica_groups=mesh['grp'=16,'tp'=8] {'grp','tp'}, dimensions={0} | all-to-all | bytes 2097152 | tf_op jit(solution)/shard_map/all_to_all | solution.py:36
  296.5 0.7 reduce_max.9
  297.1 0.7 fusion.4
  297.9 1.2 subtract_subtract_fusion
  (2 shorter events, 0.0 us)
